TPU v7x, 512 devices: a whole 4x8x8 slice. The times are simulated.
512 devices in a mesh: blk: 128 (over y_hi, x, z, core), win: 4 (over y_lo).
Axes of the slice: x: 4, y: 8 (y_hi: 2, y_lo: 4; y = y_hi * 4 + y_lo), z: 8, core: 2. Of those that a mesh axis runs over, the one named last changes fastest.
Arguments:
- records: bfloat16 [8, 3, 512, 4096], P('win', None, 'blk'), may hold values from -6 to 6
- station_row: int32 [512], replicated, may hold values from 0 to 511, each once
- pair_list: int32 [4096, 2], P('blk'), may hold values from 0 to 511
- keep_mask: int32 [8, 4096], P('win', 'blk'), may hold values 0 or 1
- azimuth: float32 [2, 4096], P(None, ('blk', 'win')), may hold values from -3.140625 to 3.140625
Outputs:
- correlation: bfloat16 [4096, 9, 4096], P(('blk', 'win'))
Inputs may be any that keep to these rules, and one draw needn't show every extreme that they name: `station_row`: each row index once.
All inputs are finite; a program needn't handle non-finite values. No bound on the sum of `keep_mask` on one device may be relied on, other than what follows from the above.
Results may differ from a plain program's by a relative error of at most 0.0075.
Values may be sent and summed in bfloat16 or wider, within the bound.
A program may use at most 64 MiB of HBM per device.

v0:
```python
import math

import jax
import jax.numpy as jnp
import numpy as np
from jax import lax
from jax.experimental import pallas as pl
from jax.experimental.pallas import tpu as pltpu
from jax.sharding import PartitionSpec as P

NT = 4096
NF = 512
FLO = 16
SMOOTH = 11
NL = 4096
QUARTER = 1024
EPSILON = 1e-05

RESIDUE = (0, 0, 2, 2, 1, 1, 3, 3)
MESH = pl.DeviceIdType.MESH


def bin_order():
    place = np.arange(64)
    return np.stack([4 * ((block % 2) * 64 + place) + RESIDUE[block] for block in range(8)])


def tables():
    bins = bin_order()
    samples = np.arange(QUARTER)

    def phase(bin_ids, times):
        return (2.0 * math.pi / NT) * ((bin_ids[..., None] + FLO) * times % NT)

    ahead = phase(bins, samples)
    forward = np.concatenate([np.cos(ahead), -np.sin(ahead)], axis=1).reshape(2 * NF, QUARTER).T
    back = phase(bins, samples - NL // 2 + NT)
    back = back.reshape(8, 8, 8, QUARTER)
    inverse = np.stack([np.cos(back), -np.sin(back)], axis=2).reshape(2 * NF, QUARTER)
    flat = bins.reshape(-1)
    apart = np.abs(flat[:, None] - flat[None, :])
    near = np.minimum(apart, NF - apart) <= SMOOTH
    return (
        jnp.asarray(forward.astype(jnp.bfloat16)),
        jnp.asarray(near.astype(jnp.bfloat16)),
        jnp.asarray(inverse.astype(jnp.bfloat16)),
    )


def dot(left, right):
    return jnp.dot(left, right, preferred_element_type=jnp.float32)


def split(value):
    lead = value.astype(jnp.bfloat16).astype(jnp.float32)
    return jnp.concatenate([lead, value - lead], axis=0).astype(jnp.bfloat16)


def lanes(shape):
    return lax.broadcasted_iota(jnp.int32, shape, len(shape) - 1)


def swap_groups(vecs, group):
    vecs = list(vecs)
    lane_group = lanes(vecs[0].shape) // group
    for step in (1, 2, 4):
        high = (lane_group // step) % 2 == 1
        for i in range(8):
            if i & step:
                continue
            low_vec, high_vec = vecs[i], vecs[i + step]
            vecs[i] = jnp.where(high, pltpu.roll(high_vec, group * step, 1), low_vec)
            vecs[i + step] = jnp.where(high, high_vec, pltpu.roll(low_vec, 128 - group * step, 1))
    return vecs


def kernel(
    rec_hbm, station_hbm, pair_hbm, keep_hbm, angle_hbm, fwd_hbm, near_hbm, inv_hbm, out_ref,
    rec_ref, station_ref, pair_ref, keep_ref, angle_ref,
    rows32, fwd, near, inv, send_a, recv_a, send_b, recv_b, full, joined, onehot,
    send_c, recv_c, send_d, recv_d,
    tab_sem, a_s, a_r, b_s, b_r, z_s, z_r, c_s, c_r, d_s, d_r,
):
    blk = lax.axis_index("blk")
    win = lax.axis_index("win")
    y_hi, x = lax.div(blk, 64), lax.rem(lax.div(blk, 16), 4)
    z, core = lax.rem(lax.div(blk, 2), 8), lax.rem(blk, 2)
    a, b = x * 2 + core, y_hi * 4 + win

    at_a, at_b, at_z = {}, {}, {}
    for k in range(1, 8):
        other = lax.rem(a + k, 8)
        at_a[k] = other, (y_hi * 64 + lax.div(other, 2) * 16 + z * 2 + lax.rem(other, 2), win)
        other = lax.rem(b + k, 8)
        at_b[k] = other, (blk + (lax.div(other, 4) - y_hi) * 64, lax.rem(other, 4))
    for k in (1, 2, 6, 7):
        other = lax.rem(z + k, 8)
        at_z[k] = other, (blk + (other - z) * 2, win)

    loads = [
        pltpu.make_async_copy(src, dst, tab_sem.at[i])
        for i, (src, dst) in enumerate(
            (
                (rec_hbm, rec_ref),
                (fwd_hbm, fwd),
                (near_hbm, near),
                (keep_hbm, keep_ref),
                (station_hbm, station_ref),
                (pair_hbm, pair_ref),
                (angle_hbm, angle_ref),
                (inv_hbm, inv),
            )
        )
    ]
    for copy in loads[:7]:
        copy.start()

    barrier = pltpu.get_barrier_semaphore()
    for at in (at_b, at_z, at_a):
        for k in at:
            pl.semaphore_signal(barrier, inc=1, device_id=at[k][1], device_id_type=MESH)

    pending = []

    def send(src, dst, sem_s, sem_r, target):
        copy = pltpu.make_async_remote_copy(
            src_ref=src, dst_ref=dst, send_sem=sem_s, recv_sem=sem_r, device_id=target, device_id_type=MESH
        )
        copy.start()
        pending.append(copy)
        return copy

    for copy in loads[3:6]:
        copy.wait()
    lane8, lane16 = lanes((8, 128)), lanes((16, 128))
    row8 = lax.broadcasted_iota(jnp.int32, (8, 128), 0)
    zero8 = jnp.zeros((8, 128), jnp.float32)
    record = jnp.zeros((8, 128), jnp.int32)
    for p in range(8):
        for side in range(2):
            spot = jnp.logical_and(row8 == side, lane8 == p)
            record = jnp.where(spot, station_ref[pair_ref[side, win * 8 + p]], record)
    r_hi, r_x, r_z = record // 256, record // 64 % 4, record // 8 % 8
    r_c, r_s = record // 4 % 2, record % 4
    place = r_z * 64 + r_hi * 32 + (r_x * 2 + r_c) * 4 + r_s
    first_digit = (place // 16).astype(jnp.float32)
    second_digit = (place % 16).astype(jnp.float32)
    keep = jnp.concatenate([keep_ref[...].astype(jnp.float32), jnp.zeros((2, 96), jnp.float32)], axis=1)
    keep = jnp.concatenate([keep, jnp.zeros((6, 128), jnp.float32)], axis=0)
    digits = jnp.where(row8 < 6, pltpu.roll(first_digit, 4, 0), pltpu.roll(second_digit, 6, 0))
    own_table = (digits, pltpu.roll(keep, 4, 0))

    loads[0].wait()
    for w in range(2):
        for c in range(3):
            rows32[c * 8 + w * 4 : c * 8 + w * 4 + 4, :] = rec_ref[w, c].astype(jnp.float32)
    q0, q1, q2, q3 = [rows32[:, QUARTER * i : QUARTER * (i + 1)] for i in range(4)]
    s02, s13, d02, d13 = q0 + q2, q1 + q3, q0 - q2, q1 - q3
    left0, left2 = split(s02 + s13), split(s02 - s13)
    left1 = jnp.concatenate([split(d02), split(d13)], axis=0)

    loads[1].wait()
    got0 = dot(left0, fwd[:, 0:256])
    got2 = dot(left2, fwd[:, 256:512])
    got1 = dot(left1, fwd[:, 512:1024])
    even = jnp.concatenate([got0[:24] + got0[24:], got2[:24] + got2[24:]], axis=1)
    odd_a = got1[0:24] + got1[24:48]
    odd_b = got1[48:72] + got1[72:96]
    half = lanes((24, 128)) < 64
    spec = [even[:, 128 * t : 128 * t + 128] for t in range(4)]
    for t in range(4):
        turned = pltpu.roll(odd_b[:, 128 * t : 128 * t + 128], 64, 1)
        plus = half if t < 2 else jnp.logical_not(half)
        spec.append(odd_a[:, 128 * t : 128 * t + 128] + jnp.where(plus, turned, -turned))
    spec = [piece * (1.0 / math.sqrt(NT)) for piece in spec]

    low_half = row8 < 4
    half8 = lanes((8, 128)) < 64
    energy = []
    for piece in spec:
        square = piece * piece
        total = square[0:8] + square[8:16] + square[16:24]
        energy.append(total + pltpu.roll(total, 64, 1))
    energy = jnp.concatenate([jnp.where(half8, energy[2 * j], energy[2 * j + 1]) for j in range(4)], axis=1)
    loads[2].wait()
    smooth = dot(split(energy), near[...])
    smooth = smooth[0:8] + smooth[8:16]
    amp = lax.rsqrt(smooth / (3.0 * (2 * SMOOTH + 1)) + EPSILON)
    for t in range(8):
        piece = amp[:, 128 * (t // 2) : 128 * (t // 2) + 128]
        turned = pltpu.roll(piece, 64, 1)
        wide = jnp.where(half8, piece, turned) if t % 2 == 0 else jnp.where(half8, turned, piece)
        white = [spec[t][8 * c : 8 * c + 8] * wide for c in range(3)]
        for w in range(2):
            v0, v1, v2 = white if w == 0 else [pltpu.roll(value, 4, 0) for value in white]
            v1 = pltpu.roll(v1, 4, 0)
            chunk = [jnp.where(low_half, v0, v1), jnp.where(low_half, v2, own_table[w])]
            send_a[w, t] = jnp.concatenate(chunk, axis=0).astype(jnp.bfloat16)

    pl.semaphore_wait(barrier, 18)

    far_first = (4, 3, 5, 2, 6, 1, 7)
    a_copies = [[], []]
    for w in range(2):
        for k in far_first:
            other, target = at_a[k]
            a_copies[w].append(
                send(send_a.at[w, other], recv_a.at[w, a], a_s.at[8 * w + k], a_r.at[8 * w + k], target)
            )
        recv_a[w, a] = send_a[w, a]
    loads[7].start()

    b_copies = [[], []]
    for w in range(2):
        for copy in a_copies[w]:
            copy.wait_recv()
        got = [recv_a[w, i].astype(jnp.float32) for i in range(8)]
        tops, lows = [value[0:8] for value in got], [value[8:16] for value in got]
        stacked = []
        for c in range(3):
            parts = tops if c < 2 else lows
            for j in range(4):
                first, second = parts[2 * j], parts[2 * j + 1]
                if c == 1:
                    stacked.append(jnp.where(low_half, pltpu.roll(first, 4, 0), second))
                else:
                    stacked.append(jnp.where(low_half, first, pltpu.roll(second, 4, 0)))
        stacked += [zero8] * 4
        turn = jnp.concatenate(stacked, axis=0).T

        def spread(a_half, q):
            merged = zero8
            for i in range(4):
                piece = pltpu.roll(lows[4 * a_half + i], (96 + 8 * i - 8 * q) % 128, 1)
                merged = jnp.where(lane8 // 8 == 12 + i, piece, merged)
            return merged

        if w == 0:
            tail = [jnp.where(low_half, pltpu.roll(spread(0, 0), 4, 0), spread(1, 0)), zero8]
        else:
            tail = []
            for a_half in range(2):
                merged = zero8
                for q in range(4):
                    piece = spread(a_half, q)
                    piece = piece if q == 2 else pltpu.roll(piece, (2 * q + 4) % 8, 0)
                    merged = jnp.where(row8 // 2 == q, piece, merged)
                tail.append(merged)
        for i in range(8):
            send_b[w, i] = jnp.concatenate(
                [turn[8 * i : 8 * i + 8] + tail[0], turn[64 + 8 * i : 72 + 8 * i] + tail[1]], axis=0
            ).astype(jnp.bfloat16)
        for k in far_first:
            other, target = at_b[k]
            b_copies[w].append(
                send(send_b.at[w, other], recv_b.at[w, b], b_s.at[8 * w + k], b_r.at[8 * w + k], target)
            )
        recv_b[w, b] = send_b[w, b]

    def share(source, h, k, sem):
        block = full.at[source, pl.ds(96 * h, 96)]
        return send(block, block, z_s.at[sem], z_r.at[sem], at_z[k][1])

    direct = {}
    tables_got = []
    for w in range(2):
        for copy in b_copies[w]:
            copy.wait_recv()
        got = [recv_b[w, i].astype(jnp.float32) for i in range(8)]
        mine = []
        for odd in range(2):
            for c in range(3):
                out = None
                for j in range(4):
                    piece = got[4 * (j % 2) + 2 * (j // 2) + odd]
                    shift = (32 * (j - c)) % 128
                    piece = pltpu.roll(piece, shift, 1) if shift else piece
                    out = piece if out is None else jnp.where(lane16 // 32 == j, piece, out)
                mine.append(out)
        full[z, 96 * w : 96 * w + 96] = jnp.concatenate(mine, axis=0).astype(jnp.bfloat16)
        for k in (2, 6):
            direct[k, w] = share(z, w, k, len(direct))
        table = []
        for t in range(4):
            merged = zero8
            for j in range(4):
                shift = (32 + 32 * j) % 128
                here = lane8 // 32 == j
                if w == 0:
                    piece = got[2 * t + j // 2][0:8]
                    piece = pltpu.roll(piece, 4, 0) if j % 2 else piece
                    piece = pltpu.roll(piece, shift, 1) if shift else piece
                    merged = jnp.where(here, piece, merged)
                    continue
                for q in range(4):
                    piece = got[4 * (t // 2) + q][8 * (j % 2) : 8 * (j % 2) + 8]
                    down = (2 * q - 2 * (2 * t % 4 + j // 2)) % 8
                    piece = pltpu.roll(piece, down, 0) if down else piece
                    piece = pltpu.roll(piece, shift, 1) if shift else piece
                    merged = jnp.where(jnp.logical_and(here, row8 // 2 == q), piece, merged)
            table.append(merged)
        tables_got.append(table)
    z_copies = []
    for w in range(2):
        for k in (1, 7):
            direct[k, w] = share(z, w, k, len(direct))
            z_copies.append(direct[k, w])
    info, keeps = tables_got

    place_ids = lax.broadcasted_iota(jnp.int32, (512, 128), 0)
    for t in range(4):
        for side in range(2):
            place = (16.0 * info[t][side : side + 1] + info[t][2 + side : 3 + side]).astype(jnp.int32)
            at = 256 * t + 128 * side
            onehot[:, at : at + 128] = jnp.where(place_ids == place, 1.0, 0.0).astype(jnp.bfloat16)

    for h in range(2):
        for step, (k, near_k) in enumerate(((2, 1), (6, 7))):
            direct[k, h].wait_recv()
            source = at_z[8 - k][0]
            if h == step:
                z_copies.append(share(source, h, k, 8 + step))
            z_copies.append(share(source, h, near_k, 10 + 2 * h + step))
    for copy in z_copies:
        copy.wait_recv()

    def to_owner(i):
        return pltpu.make_async_remote_copy(
            src_ref=send_c.at[i],
            dst_ref=recv_c.at[b],
            send_sem=c_s.at[i],
            recv_sem=c_r.at[b],
            device_id=(blk + (i // 4 - y_hi) * 64, i % 4),
            device_id_type=MESH,
        )

    def from_source(i):
        return pltpu.make_async_remote_copy(
            src_ref=send_c.at[i],
            dst_ref=recv_c.at[i],
            send_sem=c_s.at[i],
            recv_sem=c_r.at[i],
            device_id=(blk + (i // 4 - y_hi) * 64, i % 4),
            device_id_type=MESH,
        )

    low_lanes = lanes((192, 128)) < 64
    for j in range(4):
        first, second = full[2 * j].astype(jnp.float32), full[2 * j + 1].astype(jnp.float32)
        cols = slice(128 * j, 128 * j + 128)
        joined[0, :, cols] = jnp.where(low_lanes, first, pltpu.roll(second, 64, 1)).astype(jnp.bfloat16)
        joined[1, :, cols] = jnp.where(low_lanes, pltpu.roll(first, 64, 1), second).astype(jnp.bfloat16)
    for t in range(4):
        halves = [dot(joined[i], onehot[:, 256 * t : 256 * t + 256]) for i in range(2)]
        re = [[None] * 3 for _ in range(3)]
        im = [[None] * 3 for _ in range(3)]
        for w in range(8):
            mask = jnp.broadcast_to(keeps[t][w : w + 1], (8, 128))
            both = halves[w // 4]
            base = 96 * (w % 2) + 48 * (w // 2 % 2)

            def part(c, ri, side):
                at = base + 16 * c + 8 * ri
                return both[at : at + 8, 128 * side : 128 * side + 128]

            first = [(part(c, 0, 0) * mask, part(c, 1, 0) * mask) for c in range(3)]
            second = [(part(c, 0, 1), part(c, 1, 1)) for c in range(3)]
            for c in range(3):
                for d in range(3):
                    ar, ai = first[c]
                    br, bi = second[d]
                    new_re, new_im = ar * br + ai * bi, ai * br - ar * bi
                    re[c][d] = new_re if w == 0 else re[c][d] + new_re
                    im[c][d] = new_im if w == 0 else im[c][d] + new_im
        flat = []
        for i in range(3):
            for j in range(3):
                flat += [re[i][j], im[i][j]]
        main = jnp.concatenate(flat[:16], axis=0).T
        rest = jnp.concatenate(flat[16:], axis=0).T
        rest = jnp.concatenate([rest, jnp.zeros((128, 112), jnp.float32)], axis=1)
        for half_id in range(2):
            packed = jnp.zeros((8, 128), jnp.float32)
            for i in range(8):
                piece = rest[64 * half_id + 8 * i : 64 * half_id + 8 * i + 8]
                piece = pltpu.roll(piece, 16 * i, 1) if i else piece
                packed = jnp.where(lane8 // 16 == i, piece, packed)
            send_c[2 * t + half_id] = jnp.concatenate(
                [main[64 * half_id : 64 * half_id + 64], packed, jnp.zeros((8, 128), jnp.float32)], axis=0
            ).astype(jnp.bfloat16)
            pl.when(b != 2 * t + half_id)(to_owner(2 * t + half_id).start)

    recv_c[b] = send_c[b]
    for i in range(8):
        pl.when(b != i)(from_source(i).wait_recv)
    rest = swap_groups([recv_c[i, 64:80].astype(jnp.float32)[0:8] for i in range(8)], 16)
    for pair in range(4):
        pieces = [recv_c[i, 16 * pair : 16 * pair + 16].astype(jnp.float32) for i in range(8)]
        swapped = swap_groups(pieces, 16)
        for j in range(2):
            send_d[2 * pair + j] = jnp.concatenate(
                [piece[8 * j : 8 * j + 8] for piece in swapped]
                + [rest[2 * pair + j], jnp.zeros((8, 128), jnp.float32)],
                axis=0,
            ).astype(jnp.bfloat16)
    d_copies = []
    for k in (4, 3, 5, 2, 6, 1, 7):
        other, target = at_a[k]
        d_copies.append(send(send_d.at[other], recv_d.at[a], d_s.at[k], d_r.at[k], target))
    recv_d[a] = send_d[a]

    loads[7].wait()
    loads[6].wait()
    angles = jnp.concatenate([angle_ref[...], jnp.zeros((2, 120), jnp.float32)], axis=1)
    angles = jnp.concatenate([angles, jnp.zeros((6, 128), jnp.float32)], axis=0)
    sine, cosine = jnp.sin(angles).T[0:8], jnp.cos(angles).T[0:8]
    s0, s1, c0, c1 = [
        jnp.broadcast_to(value[:, i : i + 1], (8, 128)) for value in (sine, cosine) for i in range(2)
    ]
    for copy in d_copies:
        copy.wait_recv()
    ordered = []
    for block in range(8):
        got = recv_d[block].astype(jnp.float32)
        grid = [[got[24 * i + 8 * j : 24 * i + 8 * j + 8] for j in range(3)] for i in range(3)]
        for j in range(3):
            e, n = grid[0][j], grid[1][j]
            grid[0][j], grid[1][j] = s0 * e + c0 * n, s0 * n - c0 * e
        for i in range(3):
            e, n = grid[i][0], grid[i][1]
            grid[i][0], grid[i][1] = s1 * e + c1 * n, s1 * n - c1 * e
        rotated = jnp.concatenate(grid[0] + grid[1] + grid[2] + [zero8], axis=0)
        ordered.append(rotated.astype(jnp.bfloat16).astype(jnp.float32))
    left0 = jnp.concatenate(ordered[0:2], axis=1).astype(jnp.bfloat16)
    left2 = jnp.concatenate(ordered[2:4], axis=1).astype(jnp.bfloat16)
    at_re = lanes((80, 128)) // 8 % 2 == 0
    turned = []
    for t in range(4, 8):
        re_part, im_part = pltpu.roll(ordered[t], 8, 1), pltpu.roll(ordered[t], 120, 1)
        turned.append(jnp.where(at_re, -im_part, re_part) if t < 6 else jnp.where(at_re, im_part, -re_part))
    left1 = jnp.concatenate(
        [jnp.concatenate(ordered[4:8], axis=1), jnp.concatenate(turned, axis=1)], axis=0
    ).astype(jnp.bfloat16)
    scale = 1.0 / math.sqrt(NF)
    for n in range(4):
        cols = slice(256 * n, 256 * n + 256)
        e0 = dot(left0, inv[0:256, cols])
        e2 = dot(left2, inv[256:512, cols])
        odd = dot(left1, inv[512:1024, cols])
        plus, minus = e0 + e2, e0 - e2
        odd_p, odd_n = odd[0:80], odd[80:160]
        for i, value in enumerate((plus + odd_p, minus + odd_n, plus - odd_p, minus - odd_n)):
            value = (value[0:72] * scale).reshape(9, 8, 256).astype(jnp.bfloat16)
            at = QUARTER * i + 256 * n
            out_ref[:, :, at : at + 256] = value

    for copy in pending:
        copy.wait_send()
    for i in range(8):
        pl.when(b != i)(to_owner(i).wait_send)


def on_device(records, station_row, pair_list, keep_mask, azimuth):
    forward, near, inverse = tables()
    own_pairs = azimuth.shape[1]
    bf16, f32 = jnp.bfloat16, jnp.float32
    dma = pltpu.SemaphoreType.DMA
    lagged = pl.pallas_call(
        kernel,
        out_shape=jax.ShapeDtypeStruct((9, own_pairs, NL), bf16),
        in_specs=[pl.BlockSpec(memory_space=pltpu.HBM)] * 8,
        out_specs=pl.BlockSpec(memory_space=pltpu.VMEM),
        scratch_shapes=[
            pltpu.VMEM(records.shape, bf16),
            pltpu.SMEM(station_row.shape, jnp.int32),
            pltpu.SMEM(pair_list.shape[::-1], jnp.int32),
            pltpu.VMEM(keep_mask.shape, jnp.int32),
            pltpu.VMEM(azimuth.shape, f32),
            pltpu.VMEM((24, NT), f32),
            pltpu.VMEM((QUARTER, 2 * NF), bf16),
            pltpu.VMEM((NF, NF), bf16),
            pltpu.VMEM((2 * NF, QUARTER), bf16),
            pltpu.VMEM((2, 8, 16, 128), bf16),
            pltpu.VMEM((2, 8, 16, 128), bf16),
            pltpu.VMEM((2, 8, 16, 128), bf16),
            pltpu.VMEM((2, 8, 16, 128), bf16),
            pltpu.VMEM((8, 192, 128), bf16),
            pltpu.VMEM((2, 192, 512), bf16),
            pltpu.VMEM((512, 1024), bf16),
            pltpu.VMEM((8, 80, 128), bf16),
            pltpu.VMEM((8, 80, 128), bf16),
            pltpu.VMEM((8, 80, 128), bf16),
            pltpu.VMEM((8, 80, 128), bf16),
            dma((8,)),
        ]
        + [dma((16,))] * 4
        + [dma((14,))] * 2
        + [dma((8,))] * 4,
        compiler_params=pltpu.CompilerParams(
            collective_id=0, has_side_effects=True, vmem_limit_bytes=48 << 20
        ),
        name="correlate",
    )(
        *[
            pltpu.with_memory_space_constraint(operand, pltpu.HBM)
            for operand in (records, station_row, pair_list.T, keep_mask, azimuth, forward, near, inverse)
        ]
    )
    return jnp.transpose(lagged, (1, 0, 2))


def solution(mesh):
    in_specs = (
        P("win", None, "blk", None),
        P(),
        P("blk", None),
        P("win", "blk"),
        P(None, ("blk", "win")),
    )
    out_specs = P(("blk", "win"), None, None)
    return jax.shard_map(
        on_device, mesh=mesh, in_specs=in_specs, out_specs=out_specs, check_vma=False
    )
```

profile of v0, /device:TPU:1, one launch (start us, length us, event | category | flops | bytes accessed | tf_op | source)
XLA Modules:
  0.0 44.6 jit_solution(7748624021877648960)
XLA Ops:
  0.0 43.8 %correlate.1 = bf16[9,8,4096]{2,1,0:T(8,128)(2,1)S(1)} custom-call(bf16[2,3,4,4096]{3,2,1,0:T(4,128)(2,1)} %rec_hbm.1, s32[512]{0:T(512)} %station_hbm.1, s32[2,32]{1,0:T(2,128)} %bitcast.3, s32[2,32]{1,0:T(2,128)} %keep_hbm.1, f32[2,8]{1,0:T(2,128)} %angle_hbm.1, bf16[1024,1024]{1,0:T(8,128)(2,1)} %constant.6.clone.fwd_hbm, ...), custom_call_target="tpu_custom_call" | custom-call | tf_op jit(solution)/shard_map/correlate/pallas_call | solution.py:468
  43.8 0.8 %copy.10 = bf16[8,9,4096]{2,0,1:T(8,128)(2,1)} copy(bf16[8,9,4096]{2,0,1:T(8,128)(2,1)S(1)} %bitcast.2) | data formatting | bytes 1179648
where the time goes:
time: 44.7 us; the launch traced here: 44.6 us
  Pallas kernels  43.8 us (98%)
  local copies, waits for them, and re-layouts  0.82 us (2%)
    pallas_call x1, Pallas kernels, on_device(): pl.pallas_call(kernel, out_shape=jax.ShapeDtypeStruct((9, own_pairs, NL),...  43.8 us

commit v1 on v0

--- a/solution.py
+++ b/solution.py
@@ -112,11 +112,8 @@
             )
         )
     ]
-    for copy in loads[:7]:
-        copy.start()
-
     barrier = pltpu.get_barrier_semaphore()
-    for at in (at_b, at_z, at_a):
+    for at in (at_z, at_b, at_a):
         for k in at:
             pl.semaphore_signal(barrier, inc=1, device_id=at[k][1], device_id_type=MESH)
 
@@ -129,6 +126,9 @@
         copy.start()
         pending.append(copy)
         return copy
+
+    for copy in loads[:7]:
+        copy.start()
 
     for copy in loads[3:6]:
         copy.wait()
@@ -318,9 +318,9 @@
         for step, (k, near_k) in enumerate(((2, 1), (6, 7))):
             direct[k, h].wait_recv()
             source = at_z[8 - k][0]
+            z_copies.append(share(source, h, near_k, 10 + 2 * h + step))
             if h == step:
                 z_copies.append(share(source, h, k, 8 + step))
-            z_copies.append(share(source, h, near_k, 10 + 2 * h + step))
     for copy in z_copies:
         copy.wait_recv()
 

time: 44.7 us -> 44.3 us (level)
  no operation moved by 1% of the time
where the time goes in v1:
time: 44.3 us; the launch traced here: 44.2 us
  Pallas kernels  43.4 us (98%)
  local copies, waits for them, and re-layouts  0.82 us (2%)
    pallas_call x1, Pallas kernels, on_device(): pl.pallas_call(kernel, out_shape=jax.ShapeDtypeStruct((9, own_pairs, NL),...  43.4 us

profile of v1, /device:TPU:1, one launch (start us, length us, event | category | flops | bytes accessed | tf_op | source)
XLA Modules:
  0.0 44.2 jit_solution(14087877565896245005)
XLA Ops:
  0.0 43.4 %correlate.1 = bf16[9,8,4096]{2,1,0:T(8,128)(2,1)S(1)} custom-call(bf16[2,3,4,4096]{3,2,1,0:T(4,128)(2,1)} %rec_hbm.1, s32[512]{0:T(512)} %station_hbm.1, s32[2,32]{1,0:T(2,128)} %bitcast.3, s32[2,32]{1,0:T(2,128)} %keep_hbm.1, f32[2,8]{1,0:T(2,128)} %angle_hbm.1, bf16[1024,1024]{1,0:T(8,128)(2,1)} %constant.6.clone.fwd_hbm, ...), custom_call_target="tpu_custom_call" | custom-call | tf_op jit(solution)/shard_map/correlate/pallas_call | solution.py:468
  43.4 0.8 %copy.10 = bf16[8,9,4096]{2,0,1:T(8,128)(2,1)} copy(bf16[8,9,4096]{2,0,1:T(8,128)(2,1)S(1)} %bitcast.2) | data formatting | bytes 1179648

commit v2 on v1

--- a/solution.py
+++ b/solution.py
@@ -280,6 +280,8 @@
         full[z, 96 * w : 96 * w + 96] = jnp.concatenate(mine, axis=0).astype(jnp.bfloat16)
         for k in (2, 6):
             direct[k, w] = share(z, w, k, len(direct))
+        if w == 1:
+            z_copies = [share(z, h, k, 4 + 2 * h + side) for h in range(2) for side, k in enumerate((1, 7))]
         table = []
         for t in range(4):
             merged = zero8
@@ -300,19 +302,7 @@
                     merged = jnp.where(jnp.logical_and(here, row8 // 2 == q), piece, merged)
             table.append(merged)
         tables_got.append(table)
-    z_copies = []
-    for w in range(2):
-        for k in (1, 7):
-            direct[k, w] = share(z, w, k, len(direct))
-            z_copies.append(direct[k, w])
     info, keeps = tables_got
-
-    place_ids = lax.broadcasted_iota(jnp.int32, (512, 128), 0)
-    for t in range(4):
-        for side in range(2):
-            place = (16.0 * info[t][side : side + 1] + info[t][2 + side : 3 + side]).astype(jnp.int32)
-            at = 256 * t + 128 * side
-            onehot[:, at : at + 128] = jnp.where(place_ids == place, 1.0, 0.0).astype(jnp.bfloat16)
 
     for h in range(2):
         for step, (k, near_k) in enumerate(((2, 1), (6, 7))):
@@ -321,6 +311,13 @@
             z_copies.append(share(source, h, near_k, 10 + 2 * h + step))
             if h == step:
                 z_copies.append(share(source, h, k, 8 + step))
+    place_ids = lax.broadcasted_iota(jnp.int32, (512, 128), 0)
+    for t in range(4):
+        for side in range(2):
+            place = (16.0 * info[t][side : side + 1] + info[t][2 + side : 3 + side]).astype(jnp.int32)
+            at = 256 * t + 128 * side
+            onehot[:, at : at + 128] = jnp.where(place_ids == place, 1.0, 0.0).astype(jnp.bfloat16)
+
     for copy in z_copies:
         copy.wait_recv()
 

time: 44.3 us -> 44.3 us (level)
  no operation moved by 1% of the time
where the time goes in v2:
time: 44.3 us; the launch traced here: 44.1 us
  Pallas kernels  43.3 us (98%)
  local copies, waits for them, and re-layouts  0.82 us (2%)
    pallas_call x1, Pallas kernels, on_device(): pl.pallas_call(kernel, out_shape=jax.ShapeDtypeStruct((9, own_pairs, NL),...  43.3 us

profile of v2, /device:TPU:1, one launch (start us, length us, event | category | flops | bytes accessed | tf_op | source)
XLA Modules:
  0.0 44.1 jit_solution(13989242314094588580)
XLA Ops:
  0.0 43.3 %correlate.1 = bf16[9,8,4096]{2,1,0:T(8,128)(2,1)S(1)} custom-call(bf16[2,3,4,4096]{3,2,1,0:T(4,128)(2,1)} %rec_hbm.1, s32[512]{0:T(512)} %station_hbm.1, s32[2,32]{1,0:T(2,128)} %bitcast.3, s32[2,32]{1,0:T(2,128)} %keep_hbm.1, f32[2,8]{1,0:T(2,128)} %angle_hbm.1, bf16[1024,1024]{1,0:T(8,128)(2,1)} %constant.6.clone.fwd_hbm, ...), custom_call_target="tpu_custom_call" | custom-call | tf_op jit(solution)/shard_map/correlate/pallas_call | solution.py:465
  43.3 0.8 %copy.10 = bf16[8,9,4096]{2,0,1:T(8,128)(2,1)} copy(bf16[8,9,4096]{2,0,1:T(8,128)(2,1)S(1)} %bitcast.2) | data formatting | bytes 1179648
